TPU v7x, 256 devices: a whole 4x4x8 slice. The times are simulated.
256 devices in a mesh: gx: 8 (over z_lo, core), gy: 32 (over z_hi, y, x).
Axes of the slice: x: 4, y: 4, z: 8 (z_hi: 2, z_lo: 4; z = z_hi * 4 + z_lo), core: 2. Of those that a mesh axis runs over, the one named last changes fastest.
Arguments:
- features: bfloat16 [8, 512, 64, 128], P('gx', 'gy'), may hold values from -6 to 6
- block_at: int32 [64, 256, 16], P('gx', 'gy'), may hold values from -1 to 15, as said below
- block_coords: int32 [8, 3, 512], P('gx', None, 'gy'), may hold values from 0 to 15, as said below
- weight: bfloat16 [3456, 128], P('gy'), may hold values from -0.109375 to 0.109375
- cotangent: bfloat16 [8, 512, 64, 128], P('gx', 'gy'), may hold values from -6 to 6
Outputs:
- output: bfloat16 [8, 512, 64, 128], P('gx', 'gy')
- grad_features: bfloat16 [8, 512, 64, 128], P('gx', 'gy')
- grad_weight: float32 [3456, 128], P('gy')
Inputs may be any that keep to these rules, and one draw needn't show every extreme that they name: `block_at`: each entry is the slot, among the 16 slots of the device owning that position, of the active block placed there, or -1 for an empty position. A slot appears at most once in a tile; every tile has between 8 and 16 active slots, and some tile has all 16 active. `block_coords`: for each slot, its block position (first, second, third coordinate) within its device's 8 x 8 x 16 tile; the positions of one tile's slots are distinct, and a slot is active exactly when block_at at its position holds it (otherwise the position is empty).
All inputs are finite; a program needn't handle non-finite values.
Results may differ from a plain program's by a relative error of at most 0.001.
Values may be sent and summed in bfloat16 or wider, within the bound.
A program may use at most 128 MiB of HBM per device.

v0:
```python
import functools
import math

import jax
import jax.numpy as jnp
from jax import lax
from jax.experimental import pallas as pl
from jax.experimental.pallas import tpu as pltpu
from jax.sharding import PartitionSpec as P

MESH = pl.DeviceIdType.MESH
F32 = jnp.float32
BF16 = jnp.bfloat16
CH = 128
NB = 16
TAPS = 27
NOWHERE = -1.0e6
AROUND = [(dx, dy) for dx in (-1, 0, 1) for dy in (-1, 0, 1) if dx or dy]


def iota(shape, dim):
    return lax.broadcasted_iota(jnp.int32, shape, dim)


def zero_one(mask):
    return jnp.where(mask, 1.0, 0.0).astype(BF16)


def exact_dot(left, right):
    return jnp.dot(left, right, preferred_element_type=F32)


def face_slot(dx, dy):
    if dy == 0:
        return True, 0 if dx > 0 else 1
    if dx == 0:
        return True, 2 if dy > 0 else 3
    return False, (0 if dx > 0 else 2) + (0 if dy > 0 else 1)


def kernel(
    gx_size,
    gy_size,
    side,
    f_hbm,
    at_hbm,
    coords_hbm,
    w_hbm,
    g_hbm,
    out_ref,
    gf_ref,
    gw_ref,
    f_ref,
    at_ref,
    coords_ref,
    w_ref,
    g_ref,
    field_u,
    field_g,
    send_face,
    send_diag,
    halo_face,
    halo_diag,
    send_gface,
    send_gdiag,
    halo_gface,
    halo_gdiag,
    w_pair,
    w_parts,
    w_full,
    w_turned,
    dw_full,
    dw_parts,
    swap_in,
    chip_sum,
    one_in,
    one_sum,
    two_in,
    plane_sum,
    z_in,
    pieces,
    in_sem,
    hu_send,
    hu_recv,
    hg_send,
    hg_recv,
    wz_sem,
    wp_send,
    wp_recv,
    ws_sem,
    r0_send,
    r0_recv,
    r1_send,
    r1_recv,
    r2_send,
    r2_recv,
    r3_send,
    r3_recv,
    r4_send,
    r4_recv,
):
    plane = side * side
    z_low = gx_size // 2
    z_all = 2 * z_low
    rows = TAPS * CH // gy_size
    half = rows // 2
    half_pad = plane_sum.shape[1]
    piece = pieces.shape[1]
    p = lax.axis_index("gx")
    q = lax.axis_index("gy")
    core = lax.rem(p, 2)
    zlo = p // 2
    zhi = q // plane
    spot = lax.rem(q, plane)
    zed = zhi * z_low + zlo
    x = lax.rem(spot, side)
    y = spot // side
    pos1 = x + core * (y - x)
    pos2 = y + core * (x - y)
    step1 = 1 + core * (side - 1)
    step2 = side - core * (side - 1)

    sibling = (p + 1 - 2 * core, q)
    partner = (p, spot + (1 - zhi) * plane)
    ones = [lax.rem(pos1 + k, side) for k in range(1, side)]
    twos = [lax.rem(pos2 + k, side) for k in range(1, side)]
    peers1 = [(p, zhi * plane + n * step1 + pos2 * step2) for n in ones]
    peers2 = [(p, zhi * plane + pos1 * step1 + n * step2) for n in twos]
    plane_peers = []
    for k in range(1, plane):
        n1, n2 = lax.rem(pos1 + k % side, side), lax.rem(pos2 + k // side, side)
        plane_peers.append((p, zhi * plane + n1 * step1 + n2 * step2))
    zeds = [lax.rem(zed + k, z_all) for k in range(1, z_all)]
    z_peers = [(lax.rem(z, z_low) * 2 + core, (z // z_low) * plane + spot) for z in zeds]
    gx_peers = [(lax.rem(p + k, gx_size), q) for k in range(1, gx_size)]

    def at(dx, dy):
        return (lax.rem(p + dx + gx_size, gx_size), lax.rem(q + dy + gy_size, gy_size))

    def inside(dx, dy):
        return (p + dx >= 0) & (p + dx < gx_size) & (q + dy >= 0) & (q + dy < gy_size)

    barrier = pltpu.get_barrier_semaphore()
    greeted = [sibling, partner] + plane_peers + z_peers + gx_peers
    greeted = greeted + [at(dx, dy) for dx, dy in AROUND]
    for device in greeted:
        pl.semaphore_signal(barrier, inc=1, device_id=device, device_id_type=MESH)
    loads = []
    pairs = ((at_hbm, at_ref), (coords_hbm, coords_ref), (f_hbm, f_ref), (g_hbm, g_ref), (w_hbm, w_ref))
    for index, (src, dst) in enumerate(pairs):
        copy = pltpu.make_async_copy(src, dst, in_sem.at[index])
        copy.start()
        loads.append(copy)

    loads[0].wait()
    loads[1].wait()
    lane_slot = lax.rem(iota((1, CH), 1), NB).astype(F32)
    found = jnp.zeros((at_ref.shape[0], CH), F32)
    placed = at_ref[...].astype(F32)
    for z in range(placed.shape[1]):
        found = jnp.maximum(found, jnp.where(placed[:, z : z + 1] == lane_slot, 1.0, 0.0))
    live = jnp.max(found, axis=0, keepdims=True)
    spread = zero_one(lax.rem(iota((NB, CH), 1), NB) == iota((NB, CH), 0))
    coords = coords_ref[:, 0, :].astype(F32).astype(BF16)
    place = exact_dot(coords, spread)
    meta = jnp.concatenate([place, live, jnp.zeros((NB - 4, CH), F32)], axis=0).astype(BF16)

    live_rows = jnp.broadcast_to(live[:, :NB], (8, NB)).astype(BF16)
    by_high = zero_one(iota((NB, NB * NB), 1) // NB == iota((NB, NB * NB), 0))
    by_low = zero_one(lax.rem(iota((NB, NB * NB), 1), NB) == iota((NB, NB * NB), 0))
    live_high = exact_dot(live_rows, by_high)[0:1]
    live_low = exact_dot(live_rows, by_low)[0:1]
    row_id = iota((NB * NB, NB * NB), 0)
    col_id = iota((NB * NB, NB * NB), 1)
    turned = (lax.rem(row_id, NB) == col_id // NB) & (row_id // NB == lax.rem(col_id, NB))
    turn = jnp.where(turned, 1.0, 0.0)
    turn_in = (turn * live_high).astype(BF16)
    turn_out = (turn * live_low).astype(BF16)

    def take_in(ref, field, faces, diags):
        for i in range(4):
            block = ref[0, :, 16 * i : 16 * i + 16, :].reshape(NB * NB, CH)
            slab = exact_dot(turn_in, block).astype(BF16).reshape(4, 4, NB, CH)
            field[i + 1, 1:5, 1:5] = slab
            for which, along in ((0, 3), (1, 0)):
                if i == along:
                    faces[which, 0:16] = slab.reshape(16, NB, CH)
                    diags[2 * which, 0:4] = slab[3]
                    diags[2 * which + 1, 0:4] = slab[0]
            faces[2, 4 * i : 4 * i + 4] = slab[3]
            faces[3, 4 * i : 4 * i + 4] = slab[0]

    loads[2].wait()
    take_in(f_ref, field_u, send_face, send_diag)
    for n in range(4):
        send_face[n, 16] = meta
        send_diag[n, 4] = meta
    loads[4].wait()
    w_pair[zhi] = jnp.zeros((w_pair.shape[1], CH), BF16)
    w_pair[zhi, 0:rows] = w_ref[...]

    def remote(src, dst, send_sem, recv_sem, device):
        return pltpu.make_async_remote_copy(
            src_ref=src,
            dst_ref=dst,
            send_sem=send_sem,
            recv_sem=recv_sem,
            device_id=device,
            device_id_type=MESH,
        )

    def push(src, dst, send_sem, recv_sem, device):
        copy = remote(src, dst, send_sem, recv_sem, device)
        copy.start()
        return copy

    def halo_copy(index, faces, diags, faces_in, diags_in, send_sem, recv_sem):
        dx, dy = AROUND[index]
        is_face, slot = face_slot(dx, dy)
        src = faces.at[slot] if is_face else diags.at[slot]
        dst = faces_in.at[slot] if is_face else diags_in.at[slot]
        return remote(src, dst, send_sem.at[index], recv_sem.at[index], at(dx, dy))

    def halo_start(*refs):
        for index, (dx, dy) in enumerate(AROUND):

            @pl.when(inside(dx, dy))
            def _():
                halo_copy(index, *refs).start()

    def halo_wait(*refs):
        for index, (dx, dy) in enumerate(AROUND):
            is_face, slot = face_slot(dx, dy)
            landed = refs[2] if is_face else refs[3]

            @pl.when(inside(-dx, -dy))
            def _():
                halo_copy(index, *refs).wait_recv()

            @pl.when(jnp.logical_not(inside(-dx, -dy)))
            def _():
                landed[slot] = jnp.zeros(landed.shape[1:], BF16)

            @pl.when(inside(dx, dy))
            def _():
                halo_copy(index, *refs).wait_send()

    pl.semaphore_wait(barrier, len(greeted))
    u_refs = (send_face, send_diag, halo_face, halo_diag, hu_send, hu_recv)
    wz_copy = push(w_pair.at[zhi], w_pair.at[zhi], wz_sem.at[0], wz_sem.at[1], partner)
    halo_start(*u_refs)
    loads[3].wait()
    take_in(g_ref, field_g, send_gface, send_gdiag)

    wz_copy.wait()
    w_parts[core, pos1, pos2] = w_pair[core]
    w_copies = []
    for k, device in enumerate(plane_peers):
        w_copies.append(
            push(
                w_pair.at[core], w_parts.at[core, pos1, pos2], wp_send.at[k], wp_recv.at[k], device
            )
        )

    halo_wait(*u_refs)
    g_refs = (send_gface, send_gdiag, halo_gface, halo_gdiag, hg_send, hg_recv)
    halo_start(*g_refs)

    def code_of(values, dx, dy):
        values = values.astype(F32)
        code = (values[0:1] + 8.0 * dx) * 1024.0 + (values[1:2] + 8.0 * dy) * 32.0 + values[2:3]
        return jnp.where(values[3:4] > 0.5, code, NOWHERE)

    codes = {(0, 0): code_of(meta, 0, 0)}
    for dx, dy in AROUND:
        is_face, slot = face_slot(-dx, -dy)
        codes[(dx, dy)] = code_of(halo_face[slot, 16] if is_face else halo_diag[slot, 4], dx, dy)
    own_place = (place[0:1] * 1024.0 + place[1:2] * 32.0 + place[2:3])[:, :NB]
    diagonal = iota((NB, NB), 0) == iota((NB, NB), 1)
    own_code = jnp.sum(jnp.where(diagonal, own_place, 0.0), axis=1, keepdims=True)

    picks = {}
    for ax in (-1, 0, 1):
        for ay in (-1, 0, 1):
            tiles = [(dx, dy) for dx in ((0, ax) if ax else (0,)) for dy in ((0, ay) if ay else (0,))]
            depth = NB * len(tiles)
            group = iota((1, depth), 1) // NB
            code_row = codes[tiles[0]][:, :depth]
            for n in range(1, len(tiles)):
                code_row = jnp.where(group == n, codes[tiles[n]][:, :depth], code_row)
            matches = []
            for oz in (-1, 0, 1):
                for ox, oy in tiles:
                    wanted = own_code + float(ox * 1024 + oy * 32 + oz)
                    matches.append(jnp.where(wanted == code_row, 1.0, 0.0))
            picks[(ax, ay)] = (tiles, jnp.concatenate(matches, axis=0).astype(BF16))

    def padded(cell, shift):
        return 0 if shift < 0 else (5 if shift > 0 else cell + 1)

    def assemble(field, faces, diags):
        def source(dx, dy, i, j, k):
            if dx == 0 and dy == 0:
                return field[i + 1, j + 1, k + 1]
            is_face, slot = face_slot(-dx, -dy)
            if not is_face:
                return diags[slot, k]
            return faces[slot, (j if dy == 0 else i) * 4 + k]

        for (ax, ay), (tiles, pick) in picks.items():
            count = len(tiles)
            for i in {-1: (3,), 0: (1, 2), 1: (0,)}[ax]:
                for j in {-1: (3,), 0: (1, 2), 1: (0,)}[ay]:
                    for k in range(4):
                        shifts = {0: (0, 1), 3: (-1, 0)}.get(k, (0,))
                        if count == 1 and k in (1, 2):
                            continue
                        first = (shifts[0] + 1) * count * NB
                        last = (shifts[-1] + 2) * count * NB
                        pool = [source(dx, dy, i, j, k) for dx, dy in tiles]
                        pool = pool[0] if count == 1 else jnp.concatenate(pool, axis=0)
                        got = exact_dot(pick[first:last], pool).astype(BF16)
                        row = 0
                        for oz in shifts:
                            for ox, oy in tiles:
                                if ox or oy or oz:
                                    to = padded(i, ox), padded(j, oy), padded(k, oz)
                                    field[to] = got[row : row + NB]
                                row += NB

    assemble(field_u, halo_face, halo_diag)

    def window(field, tap):
        a, b, e = tap // 9, tap // 3 % 3, tap % 3
        return field[a : a + 4, b : b + 4, e : e + 4].reshape(1024, CH)

    kept_turned = field_g[1:5, 1:5, 1:5].reshape(1024, CH).T
    dw_full[TAPS * CH :] = jnp.zeros((dw_full.shape[0] - TAPS * CH, CH), F32)

    def gradient(first, last):
        for tap in range(first, last, 2):
            upto = min(tap + 2, last)
            right = [window(field_u, n) for n in range(tap, upto)]
            right = right[0] if len(right) == 1 else jnp.concatenate(right, axis=1)
            dw_full[tap * CH : upto * CH] = exact_dot(kept_turned, right).T

    def split(which):
        for n in range(plane):
            for part in range(2):
                start = (which * plane + n) * rows + part * half
                nx, ny = n % side, n // side
                to = (nx, ny) if part == 0 else (ny, nx)
                dw_parts[part, which, to[0], to[1]] = dw_full[start : start + half_pad]
        return push(
            dw_parts.at[1 - core, which],
            swap_in.at[which],
            r0_send.at[which],
            r0_recv.at[which],
            sibling,
        )

    def phase_one(which, swap):
        swap.wait()
        chip_sum[which] = dw_parts[core, which] + swap_in[which]
        copies = []
        for k, device in enumerate(peers1):
            index = which * (side - 1) + k
            copies.append(
                push(
                    chip_sum.at[which, ones[k]],
                    one_in.at[which, k],
                    r1_send.at[index],
                    r1_recv.at[index],
                    device,
                )
            )
        return copies

    def phase_two(which, arriving):
        for copy in arriving:
            copy.wait()
        total = chip_sum[which, pos1]
        for k in range(side - 1):
            total = total + one_in[which, k]
        one_sum[which] = total
        copies = []
        for k, device in enumerate(peers2):
            index = which * (side - 1) + k
            copies.append(
                push(
                    one_sum.at[which, twos[k]],
                    two_in.at[which, k],
                    r2_send.at[index],
                    r2_recv.at[index],
                    device,
                )
            )
        return copies

    def phase_done(which, arriving):
        for copy in arriving:
            copy.wait()
        total = one_sum[which, pos2]
        for k in range(side - 1):
            total = total + two_in[which, k]
        plane_sum[which] = total

    gradient(0, 14)
    swap_low = split(0)
    gradient(14, TAPS)
    swap_high = split(1)
    one_low = phase_one(0, swap_low)
    one_high = phase_one(1, swap_high)
    for copy in w_copies:
        copy.wait()
    ws_copy = push(w_parts.at[core], w_parts.at[core], ws_sem.at[0], ws_sem.at[1], sibling)
    def convolve(field, weights, result_ref, i):
        total = None
        for tap in range(0, TAPS, 2):
            last = min(tap + 2, TAPS)
            left = []
            for n in range(tap, last):
                a, b, e = n // 9, n // 3 % 3, n % 3
                left.append(field[i + a, b : b + 4, e : e + 4].reshape(256, CH))
            left = left[0] if len(left) == 1 else jnp.concatenate(left, axis=1)
            term = exact_dot(left, weights[tap * CH : last * CH])
            total = term if total is None else total + term
        slab = exact_dot(turn_out, total.astype(BF16)).astype(BF16)
        result_ref[0, :, 16 * i : 16 * i + 16, :] = slab.reshape(NB, 16, CH)

    two_low = phase_two(0, one_low)
    two_high = phase_two(1, one_high)
    ws_copy.wait()
    for which in range(2):
        for n in range(plane):
            nx, ny = n % side, n // side
            to = (nx, ny) if which == 0 else (ny, nx)
            start = (which * plane + n) * rows
            w_full[start : start + rows] = w_parts[which, to[0], to[1], 0:rows]
    for tap in range(TAPS):
        w_turned[(26 - tap) * CH : (27 - tap) * CH] = w_full[tap * CH : (tap + 1) * CH].T

    for i in range(0, 2):
        convolve(field_u, w_full, out_ref, i)
    phase_done(0, two_low)
    phase_done(1, two_high)

    def piece_start(low):
        start = low * piece
        return pl.multiple_of(jnp.minimum(start, half_pad - piece), 8)

    z_copies = []
    for k, device in enumerate(z_peers):
        low = lax.rem(zeds[k], z_low)
        z_copies.append(
            push(
                plane_sum.at[zeds[k] // z_low, pl.ds(piece_start(low), piece)],
                z_in.at[k],
                r3_send.at[k],
                r3_recv.at[k],
                device,
            )
        )
    for i in range(2, 4):
        convolve(field_u, w_full, out_ref, i)
    halo_wait(*g_refs)
    assemble(field_g, halo_gface, halo_gdiag)
    for copy in z_copies:
        copy.wait()
    total = plane_sum[zhi, pl.ds(piece_start(zlo), piece)]
    for k in range(z_all - 1):
        total = total + z_in[k]
    pieces[p] = total * (1.0 / math.sqrt(gx_size * gy_size * NB * 64))
    last_copies = []
    for k, device in enumerate(gx_peers):
        last_copies.append(push(pieces.at[p], pieces.at[p], r4_send.at[k], r4_recv.at[k], device))
    for i in range(0, 4):
        convolve(field_g, w_turned, gf_ref, i)
    for copy in last_copies:
        copy.wait()
    for n in range(gx_size):
        part, low = n % 2, n // 2
        start = min(low * piece, half_pad - piece)
        count = min(piece, half - start)
        gw_ref[part * half + start : part * half + start + count] = pieces[n, 0:count]


def deliver(a_ref, b_ref, c_ref, a_out, b_out, c_out):
    a_out[...] = a_ref[...]
    b_out[...] = b_ref[...]
    c_out[...] = c_ref[...]


def hand_over(*arrays):
    return pl.pallas_call(
        deliver,
        out_shape=tuple(jax.ShapeDtypeStruct(a.shape, a.dtype) for a in arrays),
        in_specs=[pl.BlockSpec(memory_space=pltpu.VMEM)] * 3,
        out_specs=[pl.BlockSpec(memory_space=pltpu.VMEM)] * 3,
    )(*arrays)


def local(gx_size, gy_size, features, block_at, block_coords, weight, cotangent):
    plane = gy_size // 2
    side = math.isqrt(plane)
    z_low = gx_size // 2
    z_all = 2 * z_low
    rows = TAPS * CH // gy_size
    rows_pad = -(-rows // 16) * 16
    half_pad = -(-(rows // 2) // 8) * 8
    piece = -(-half_pad // (8 * z_low)) * 8
    blocks = pl.BlockSpec(memory_space=pltpu.VMEM)
    vmem = pltpu.VMEM
    dma = pltpu.SemaphoreType.DMA
    corners = block_coords.transpose(1, 0, 2)
    positions = block_at.reshape(-1, block_at.shape[2])
    results = pl.pallas_call(
        functools.partial(kernel, gx_size, gy_size, side),
        out_shape=(
            jax.ShapeDtypeStruct(features.shape, BF16),
            jax.ShapeDtypeStruct(features.shape, BF16),
            jax.ShapeDtypeStruct((rows, CH), F32),
        ),
        in_specs=[pl.BlockSpec(memory_space=pl.ANY)] * 5,
        out_specs=[blocks] * 3,
        scratch_shapes=[
            vmem(features.shape, BF16),
            vmem(positions.shape, jnp.int32),
            vmem(corners.shape, jnp.int32),
            vmem(weight.shape, BF16),
            vmem(features.shape, BF16),
            vmem((6, 6, 6, NB, CH), BF16),
            vmem((6, 6, 6, NB, CH), BF16),
            vmem((4, 17, NB, CH), BF16),
            vmem((4, 5, NB, CH), BF16),
            vmem((4, 17, NB, CH), BF16),
            vmem((4, 5, NB, CH), BF16),
            vmem((4, 16, NB, CH), BF16),
            vmem((4, 4, NB, CH), BF16),
            vmem((4, 16, NB, CH), BF16),
            vmem((4, 4, NB, CH), BF16),
            vmem((2, rows_pad, CH), BF16),
            vmem((2, side, side, rows_pad, CH), BF16),
            vmem((TAPS * CH, CH), BF16),
            vmem((TAPS * CH, CH), BF16),
            vmem((TAPS * CH + 16, CH), F32),
            vmem((2, 2, side, side, half_pad, CH), F32),
            vmem((2, side, side, half_pad, CH), F32),
            vmem((2, side, side, half_pad, CH), F32),
            vmem((2, side - 1, side, half_pad, CH), F32),
            vmem((2, side, half_pad, CH), F32),
            vmem((2, side - 1, half_pad, CH), F32),
            vmem((2, half_pad, CH), F32),
            vmem((z_all - 1, piece, CH), F32),
            vmem((gx_size, piece, CH), F32),
            dma((5,)),
            dma((8,)),
            dma((8,)),
            dma((8,)),
            dma((8,)),
            dma((2,)),
            dma((plane - 1,)),
            dma((plane - 1,)),
            dma((2,)),
            dma((2,)),
            dma((2,)),
            dma((2 * side - 2,)),
            dma((2 * side - 2,)),
            dma((2 * side - 2,)),
            dma((2 * side - 2,)),
            dma((z_all - 1,)),
            dma((z_all - 1,)),
            dma((gx_size - 1,)),
            dma((gx_size - 1,)),
        ],
        compiler_params=pltpu.CompilerParams(
            collective_id=0, has_side_effects=True, vmem_limit_bytes=63 * 1024 * 1024
        ),
    )(features, positions, corners, weight, cotangent)
    return hand_over(*results)


def solution(mesh):
    placed = (
        P("gx", "gy", None, None),
        P("gx", "gy", None),
        P("gx", None, "gy"),
        P("gy", None),
        P("gx", "gy", None, None),
    )
    return jax.shard_map(
        functools.partial(local, mesh.shape["gx"], mesh.shape["gy"]),
        mesh=mesh,
        in_specs=placed,
        out_specs=(P("gx", "gy", None, None), P("gx", "gy", None, None), P("gy", None)),
        check_vma=False,
    )
```

profile of v0, /device:TPU:17, one launch (start us, length us, event | category | flops | bytes accessed | tf_op | source)
XLA Modules:
  0.0 47.6 jit_solution(10425560239813709952)
XLA Ops:
  0.6 45.1 %shard_map.76 = (bf16[1,16,64,128]{3,2,1,0:T(8,128)(2,1)}, bf16[1,16,64,128]{3,2,1,0:T(8,128)(2,1)}, f32[108,128]{1,0:T(8,128)}) custom-call(bf16[1,16,64,128]{3,2,1,0:T(8,128)(2,1)} %f_hbm.1, s32[64,16]{1,0:T(8,128)} %bitcast.2, s32[3,1,16]{2,1,0:T(1,128)} %bitcast.3, bf16[108,128]{1,0:T(8,128)(2,1)} %w_hbm.1, bf16[1,16,64,128]{3,2,1,0:T(8,128)(2,1)} %g_hbm.1), custom_call_target="tpu_custom_call" | custom-call | tf_op jit(solution)/shard_map/pallas_call | solution.py:517
  45.7 1.8 %shard_map.77 = (bf16[1,16,64,128]{3,2,1,0:T(8,128)(2,1)}, bf16[1,16,64,128]{3,2,1,0:T(8,128)(2,1)}, f32[108,128]{1,0:T(8,128)}) custom-call(bf16[1,16,64,128]{3,2,1,0:T(8,128)(2,1)} %get-tuple-element.6.a_ref, bf16[1,16,64,128]{3,2,1,0:T(8,128)(2,1)} %get-tuple-element.7.b_ref, f32[108,128]{1,0:T(8,128)} %get-tuple-element.8.c_ref), custom_call_target="tpu_custom_call" | custom-call | tf_op jit(solution)/shard_map/pallas_call | solution.py:495
where the time goes:
time: 48.3 us; the launch traced here: 47.6 us
  Pallas kernels  47 us (97%)
  between operations  0.64 us (1%)
    pallas_call x1, Pallas kernels, local(): pl.pallas_call(functools.partial(kernel, gx_size, gy_size, side), out_sha...  45.1 us
    pallas_call x1, Pallas kernels, hand_over(): pl.pallas_call(deliver, out_shape=tuple((jax.ShapeDtypeStruct(a.shape, a....  1.85 us

commit v1 on v0

--- a/solution.py
+++ b/solution.py
@@ -411,9 +411,6 @@
     swap_high = split(1)
     one_low = phase_one(0, swap_low)
     one_high = phase_one(1, swap_high)
-    for copy in w_copies:
-        copy.wait()
-    ws_copy = push(w_parts.at[core], w_parts.at[core], ws_sem.at[0], ws_sem.at[1], sibling)
     def convolve(field, weights, result_ref, i):
         total = None
         for tap in range(0, TAPS, 2):
@@ -430,6 +427,9 @@
 
     two_low = phase_two(0, one_low)
     two_high = phase_two(1, one_high)
+    for copy in w_copies:
+        copy.wait()
+    ws_copy = push(w_parts.at[core], w_parts.at[core], ws_sem.at[0], ws_sem.at[1], sibling)
     ws_copy.wait()
     for which in range(2):
         for n in range(plane):

time: 48.3 us -> 49.1 us (1.017)
  the two profiles are of different devices: /device:TPU:17 before, /device:TPU:5 now
where the time goes in v1:
time: 49.1 us; the launch traced here: 49 us
  Pallas kernels  48.3 us (98%)
  between operations  0.64 us (1%)
    pallas_call x1, Pallas kernels, local(): pl.pallas_call(functools.partial(kernel, gx_size, gy_size, side), out_sha...  46.5 us
    pallas_call x1, Pallas kernels, hand_over(): pl.pallas_call(deliver, out_shape=tuple((jax.ShapeDtypeStruct(a.shape, a....  1.85 us

profile of v1, /device:TPU:5, one launch (start us, length us, event | category | flops | bytes accessed | tf_op | source)
XLA Modules:
  0.0 49.0 jit_solution(4320418841507419106)
XLA Ops:
  0.6 46.5 %shard_map.76 = (bf16[1,16,64,128]{3,2,1,0:T(8,128)(2,1)}, bf16[1,16,64,128]{3,2,1,0:T(8,128)(2,1)}, f32[108,128]{1,0:T(8,128)}) custom-call(bf16[1,16,64,128]{3,2,1,0:T(8,128)(2,1)} %f_hbm.1, s32[64,16]{1,0:T(8,128)} %bitcast.2, s32[3,1,16]{2,1,0:T(1,128)} %bitcast.3, bf16[108,128]{1,0:T(8,128)(2,1)} %w_hbm.1, bf16[1,16,64,128]{3,2,1,0:T(8,128)(2,1)} %g_hbm.1), custom_call_target="tpu_custom_call" | custom-call | tf_op jit(solution)/shard_map/pallas_call | solution.py:517
  47.1 1.8 %shard_map.77 = (bf16[1,16,64,128]{3,2,1,0:T(8,128)(2,1)}, bf16[1,16,64,128]{3,2,1,0:T(8,128)(2,1)}, f32[108,128]{1,0:T(8,128)}) custom-call(bf16[1,16,64,128]{3,2,1,0:T(8,128)(2,1)} %get-tuple-element.6.a_ref, bf16[1,16,64,128]{3,2,1,0:T(8,128)(2,1)} %get-tuple-element.7.b_ref, f32[108,128]{1,0:T(8,128)} %get-tuple-element.8.c_ref), custom_call_target="tpu_custom_call" | custom-call | tf_op jit(solution)/shard_map/pallas_call | solution.py:495
